TPU v7x, 128 devices: a whole 4x4x4 slice. The times are simulated.
128 devices in a mesh: user: 16 (over y, x_lo, core), hist: 8 (over z, x_hi).
Axes of the slice: x: 4 (x_hi: 2, x_lo: 2; x = x_hi * 2 + x_lo), y: 4, z: 4, core: 2. Of those that a mesh axis runs over, the one named last changes fastest.
Arguments:
- cand_embed: bfloat16 [32768, 1024], P(('user', 'hist')), may hold values from -6 to 6
- cand_group: int32 [32768, 1], P(('user', 'hist')), may hold values from 0 to 15; in each aligned block of 256 rows (0 to 255, 256 to 511, ...) at most 32 rows name the same one
- cand_user: int32 [32768], P(('user', 'hist')), may hold values from 0 to 3
- hist_len: int32 [64], P('user'), may hold values from 128 to 2048
- block_list: int32 [1024], P(('user', 'hist')), may hold values from 0 to 63, as said below
- hist_keys: bfloat16 [131072, 1024], P(('user', 'hist')), may hold values from -6 to 6
- hist_values: bfloat16 [131072, 1024], P(('user', 'hist')), may hold values from -6 to 6
- in_gain: float32 [1024], replicated, may hold values from 0.1 to 1.9
- w_in: bfloat16 [1024, 2048], replicated, may hold values from -0.1875 to 0.1875
- attn_gain: float32 [1024], replicated, may hold values from 0.1 to 1.9
- w_out: bfloat16 [1024, 1024], replicated, may hold values from -0.1875 to 0.1875
Outputs:
- ranked: bfloat16 [32768, 1024], P(('user', 'hist'))
Inputs may be any that keep to these rules, and one draw needn't show every extreme that they name: `cand_group`: among the 256 candidates of one device at most 32 name the same group. `block_list`: each aligned run of 64 entries, one group's blocks, holds every slot of 0 to 63 once.
All inputs are finite; a program needn't handle non-finite values.
Results may differ from a plain program's by a relative error of at most 0.0059.
Values may be sent and summed in bfloat16 or wider, within the bound.
No kernel may reach another device: no remote copies, remote signals or barrier semaphores. Data moves between devices by JAX's collectives and lax.ppermute only.
A program may use at most 192 MiB of HBM per device.

v0:
```python
import functools

import jax
import jax.numpy as jnp
from jax import lax
from jax.experimental import pallas as pl
from jax.experimental.pallas import tpu as pltpu
from jax.sharding import PartitionSpec as P

HEADS = 8
HEAD = 128
BLK = 128
BLK_USR = 16
USERS = 4
SLOTS = 32
CHUNK = 512
PAD = 16
SORTED = CHUNK + 128
COPY = 64
TILE = 256
KEYS = 1024
REST = 512
VMEM = 48 * 1024 * 1024

BF16 = jnp.bfloat16
F32 = jnp.float32


def dot(a, b, contract):
    return lax.dot_general(a, b, ((contract[0], contract[1]), ((), ())), preferred_element_type=F32)


def params():
    return pltpu.CompilerParams(vmem_limit_bytes=VMEM)


def vmem():
    return pl.BlockSpec(memory_space=pltpu.VMEM)


def smem():
    return pl.BlockSpec(memory_space=pltpu.SMEM)


def regroup_kernel(keys_ref, values_ref, out_ref):
    out_ref[0, :, :HEAD] = keys_ref[...]
    out_ref[0, :, HEAD:] = values_ref[...]


def regroup(keys, values):
    rows = keys.shape[0]
    return pl.pallas_call(
        regroup_kernel,
        grid=(HEADS,),
        out_shape=jax.ShapeDtypeStruct((HEADS, rows, 2 * HEAD), BF16),
        in_specs=[pl.BlockSpec((rows, HEAD), lambda h: (0, h))] * 2,
        out_specs=pl.BlockSpec((1, rows, 2 * HEAD), lambda h: (h, 0, 0)),
        compiler_params=params(),
        name="regroup",
    )(keys, values)


def query_kernel(
    turn_ref,
    list_ref,
    group_ref,
    user_ref,
    embed_ref,
    gain_ref,
    w_ref,
    packed_ref,
    normed_ref,
    slot_ref,
    place,
    notes,
):
    rows = embed_ref.shape[0]
    groups = packed_ref.shape[0]
    slots = groups * SLOTS

    @pl.when(pl.program_id(0) == 0)
    def _():
        group = group_ref[...]
        member = (group == lax.broadcasted_iota(jnp.int32, (groups, rows), 0)).astype(F32)
        before = (
            lax.broadcasted_iota(jnp.int32, (rows, rows), 0)
            < lax.broadcasted_iota(jnp.int32, (rows, rows), 1)
        ).astype(BF16)
        count = dot(member.astype(BF16), before, ((1,), (0,)))
        position = jnp.sum(count * member, axis=0, keepdims=True).astype(jnp.int32)
        slot = group * SLOTS + position
        slot_ref[...] = slot
        place[...] = (slot == lax.broadcasted_iota(jnp.int32, (slots, rows), 0)).astype(BF16)
        offset = turn_ref[0] * SLOTS
        lanes = lax.broadcasted_iota(jnp.int32, (HEAD, rows), 0) == position + offset
        users = member * (user_ref[...] - USERS).astype(F32)
        tags = dot(users.astype(BF16), lanes.astype(BF16), ((1,), (1,)))
        own = lax.broadcasted_iota(jnp.int32, tags.shape, 1) - offset
        tags = tags + jnp.where((own >= 0) & (own < SLOTS), USERS, 0).astype(F32)
        lane = lax.broadcasted_iota(jnp.int32, (groups, PAD, HEAD), 2)
        row = lax.broadcasted_iota(jnp.int32, (groups, PAD, HEAD), 1)
        listed = jnp.zeros((groups, PAD, HEAD), jnp.int32)
        for b in range(list_ref.shape[0]):
            listed = jnp.where(lane == b, list_ref[b], listed)
        tags = jnp.broadcast_to(tags.reshape(groups, 1, HEAD), (groups, PAD, HEAD))
        notes[...] = jnp.where(
            row == 0, tags, jnp.where(row == 1, listed.astype(F32), 0.0)
        ).astype(BF16)
        values = embed_ref[...].astype(F32)
        scaling = lax.rsqrt(jnp.mean(values * values, axis=-1, keepdims=True) + 1e-06)
        normed_ref[...] = (values * scaling * gain_ref[...]).astype(BF16)

    query = dot(normed_ref[...], w_ref[...], ((1,), (0,)))
    query = (query / (1.0 + jnp.exp(-query))).astype(BF16)
    packed = dot(place[...], query, ((1,), (0,))).astype(BF16)
    for h in range(packed_ref.shape[1]):
        packed_ref[:, h, :SLOTS] = packed[:, h * HEAD : (h + 1) * HEAD].reshape(
            groups, SLOTS, HEAD
        )
        packed_ref[:, h, SLOTS:] = notes[...]


def make_queries(turn, listed, group, user, embed, gain, w_in, groups):
    rows, width = embed.shape
    step = 2 * HEAD

    def whole(*shape):
        return pl.BlockSpec(shape, lambda i: (0,) * len(shape))

    return pl.pallas_call(
        query_kernel,
        grid=(width // step,),
        out_shape=(
            jax.ShapeDtypeStruct((groups, HEADS, SLOTS + PAD, HEAD), BF16),
            jax.ShapeDtypeStruct((rows, width), BF16),
            jax.ShapeDtypeStruct((1, rows), jnp.int32),
        ),
        in_specs=[
            smem(),
            smem(),
            whole(1, rows),
            whole(1, rows),
            whole(rows, width),
            whole(1, width),
            pl.BlockSpec((width, step), lambda i: (0, i)),
        ],
        out_specs=(
            pl.BlockSpec((groups, step // HEAD, SLOTS + PAD, HEAD), lambda i: (0, i, 0, 0)),
            whole(rows, width),
            whole(1, rows),
        ),
        scratch_shapes=[
            pltpu.VMEM((groups * SLOTS, rows), BF16),
            pltpu.VMEM((groups, PAD, HEAD), BF16),
        ],
        compiler_params=params(),
        name="make_queries",
    )(turn, listed, group, user, embed, gain.reshape(1, width), w_in)


def gate_kernel(slot_ref, normed_ref, w_ref, gate_ref, place_ref):
    rows = normed_ref.shape[0]
    gate = dot(normed_ref[...], w_ref[...], ((1,), (0,)))
    gate_ref[...] = (gate / (1.0 + jnp.exp(-gate))).astype(BF16)
    column = jnp.broadcast_to(slot_ref[...].astype(F32), (8, rows)).T[:, :1].astype(jnp.int32)
    lane = lax.broadcasted_iota(jnp.int32, place_ref.shape, 1)
    place_ref[...] = (column == lane).astype(BF16)


def make_gate(slot, normed, w_in, slots):
    rows, width = normed.shape
    return pl.pallas_call(
        gate_kernel,
        grid=(1,),
        out_shape=(
            jax.ShapeDtypeStruct((rows, width), BF16),
            jax.ShapeDtypeStruct((rows, slots), BF16),
        ),
        in_specs=[
            pl.BlockSpec((1, rows), lambda i: (0, 0)),
            pl.BlockSpec((rows, width), lambda i: (0, 0)),
            pl.BlockSpec((width, width), lambda i: (0, 1)),
        ],
        out_specs=(
            pl.BlockSpec((rows, width), lambda i: (0, 0)),
            pl.BlockSpec((rows, slots), lambda i: (0, 0)),
        ),
        compiler_params=params(),
        name="make_gate",
    )(slot, normed, w_in)


def padded(count):
    return (count + (PAD - 1)) // PAD * PAD


def bases(counts_ref, chunks):
    starts, sizes, start = [], [], jnp.int32(0)
    for u in range(USERS):
        size = jnp.int32(0)
        for c in range(chunks):
            size = size + padded(counts_ref[c, u])
        starts.append(start)
        sizes.append(size)
        start = start + size
    return starts, sizes


def copy_rows(count, source, start, target, end):
    def step(i, carry):
        rows = source[pl.ds(pl.multiple_of(start + i * COPY, PAD), COPY), :]
        target[pl.ds(pl.multiple_of(end + i * COPY, PAD), COPY), :] = rows
        return carry

    lax.fori_loop(0, (count + (COPY - 1)) // COPY, step, 0)


def runs(counts_ref, c):
    starts, start = [], jnp.int32(0)
    for u in range(USERS):
        starts.append(start)
        start = start + padded(counts_ref[c, u])
    return starts


def sort_kernel(counts_ref, tags_ref, query_ref, pick_ref, sorted_ref, chunk_ref):
    chunks = tags_ref.shape[0]
    sources = CHUNK // SLOTS
    earlier = (
        lax.broadcasted_iota(jnp.int32, (CHUNK, CHUNK), 0)
        < lax.broadcasted_iota(jnp.int32, (CHUNK, CHUNK), 1)
    ).astype(BF16)
    places = []
    for c in range(chunks):
        tags = tags_ref[c : c + 1, :]
        lanes = (tags == lax.broadcasted_iota(jnp.int32, (8, CHUNK), 0)).astype(F32)
        rank = dot(lanes.astype(BF16), earlier, ((1,), (0,))).astype(jnp.int32)
        starts = runs(counts_ref, c)
        place = jnp.full((1, CHUNK), -1, jnp.int32)
        for u in range(USERS):
            place = jnp.where(tags == u, rank[u : u + 1, :] + starts[u], place)
        places.append(place)
        pick = (lax.broadcasted_iota(jnp.int32, (SORTED, CHUNK), 0) == place).astype(BF16)
        query = query_ref[c * sources : (c + 1) * sources, :SLOTS].reshape(CHUNK, HEAD)
        chunk_ref[c * SORTED : (c + 1) * SORTED, :] = dot(pick, query, ((1,), (0,))).astype(BF16)
    chunk_ref[chunks * SORTED :, :] = jnp.zeros((COPY, HEAD), BF16)
    sorted_ref[...] = jnp.zeros_like(sorted_ref)
    row = jnp.int32(0)
    for u in range(USERS):
        for c in range(chunks):
            count = counts_ref[c, u]
            copy_rows(count, chunk_ref, c * SORTED + runs(counts_ref, c)[u], sorted_ref, row)
            row = row + padded(count)
    columns = jnp.concatenate(places, axis=0).astype(F32).T.astype(jnp.int32)
    for c in range(chunks):
        lane = lax.broadcasted_iota(jnp.int32, (CHUNK, SORTED), 1)
        pick_ref[c] = (columns[:, c : c + 1] == lane).astype(BF16)


def sort_queries(counts, tags, query):
    chunks = tags.shape[0]
    return pl.pallas_call(
        sort_kernel,
        out_shape=(
            jax.ShapeDtypeStruct((chunks, CHUNK, SORTED), BF16),
            jax.ShapeDtypeStruct((chunks * SORTED + TILE, HEAD), BF16),
        ),
        in_specs=[smem(), vmem(), vmem()],
        out_specs=(vmem(), vmem()),
        scratch_shapes=[pltpu.VMEM((chunks * SORTED + COPY, HEAD), BF16)],
        compiler_params=params(),
        name="sort_queries",
    )(counts, tags, query)


def attend_kernel(
    counts_ref,
    where_ref,
    length_ref,
    query_ref,
    pick_hbm,
    kv_hbm,
    out_ref,
    kv,
    pick,
    total,
    chunk,
    kv_sem,
    pick_sem,
):
    chunks = out_ref.shape[0]
    blocks = kv_hbm.shape[1] // BLK
    starts, sizes = bases(counts_ref, chunks)
    fetch = pltpu.make_async_copy(kv_hbm, kv, kv_sem)
    fetch.start()
    picks = pltpu.make_async_copy(pick_hbm, pick, pick_sem)
    picks.start()
    total[...] = jnp.zeros_like(total)
    chunk[...] = jnp.zeros_like(chunk)
    fetch.wait()

    scale = 0.5 * HEAD ** (-0.5)

    def partial(query, u, first, count, limit):
        parts = []
        for j in range(count):
            at = where_ref[u * BLK_USR + first + j]
            row = pl.multiple_of(at % blocks * BLK, BLK)
            parts.append(kv[at // blocks, pl.ds(row, BLK), :])
        part = jnp.concatenate(parts, axis=0)
        half = dot(query, part[:, :HEAD], ((1,), (1,))) * scale
        weight = half + half * jnp.tanh(half)
        if limit is not None:
            column = lax.broadcasted_iota(jnp.int32, weight.shape, 1)
            weight = jnp.where(column < limit, weight, 0.0)
        return dot(weight.astype(BF16), part[:, HEAD:], ((1,), (0,)))

    for u in range(USERS):
        length = length_ref[u]
        whole = length // KEYS
        rest = (length - whole * KEYS + (REST - 1)) // REST

        def tile(i, carry, u=u, length=length, whole=whole, rest=rest):
            at = pl.multiple_of(starts[u] + i * TILE, PAD)
            query = query_ref[pl.ds(at, TILE), :]

            def step(k, running):
                return running + partial(query, u, k * (KEYS // BLK), KEYS // BLK, None)

            def end(k, running):
                first = whole * KEYS + k * REST
                return running + partial(query, u, first // BLK, REST // BLK, length - first)

            running = lax.fori_loop(0, whole, step, jnp.zeros((TILE, HEAD), F32))
            running = lax.fori_loop(0, rest, end, running)
            total[pl.ds(at, TILE), :] = running.astype(BF16)
            return carry

        lax.fori_loop(0, (sizes[u] + (TILE - 1)) // TILE, tile, 0)

    picks.wait()
    rows = list(starts)
    for c in range(chunks):
        run = runs(counts_ref, c)
        for u in range(USERS):
            count = counts_ref[c, u]
            copy_rows(count, total, rows[u], chunk, c * SORTED + run[u])
            rows[u] = rows[u] + padded(count)
    for c in range(chunks):
        out_ref[c] = dot(pick[c], chunk[c * SORTED : (c + 1) * SORTED, :], ((1,), (0,))).astype(BF16)


def attend(counts, where, length, query, pick, kv):
    chunks = pick.shape[0]
    rows = query.shape[0]
    anywhere = pl.BlockSpec(memory_space=pl.ANY)
    return pl.pallas_call(
        attend_kernel,
        out_shape=jax.ShapeDtypeStruct((chunks, CHUNK, HEAD), BF16),
        in_specs=[smem(), smem(), smem(), vmem(), anywhere, anywhere],
        out_specs=vmem(),
        scratch_shapes=[
            pltpu.VMEM(kv.shape, BF16),
            pltpu.VMEM(pick.shape, BF16),
            pltpu.VMEM((rows, HEAD), BF16),
            pltpu.VMEM((chunks * SORTED + COPY, HEAD), BF16),
            pltpu.SemaphoreType.DMA,
            pltpu.SemaphoreType.DMA,
        ],
        compiler_params=params(),
        name="attend",
    )(counts, where, length, query, pick, kv)


def finish_kernel(returned_ref, place_ref, embed_ref, gate_ref, gain_ref, w_ref, out_ref, attended):
    slots = place_ref.shape[1]
    for h in range(HEADS):
        attended[:, h * HEAD : (h + 1) * HEAD] = dot(
            place_ref[...], returned_ref[:, h].reshape(slots, HEAD), ((1,), (0,))
        )
    picked = attended[...]
    scaling = lax.rsqrt(jnp.mean(picked * picked, axis=-1, keepdims=True) + 1e-05)
    gated = (picked * scaling * gain_ref[...] * gate_ref[...].astype(F32)).astype(BF16)
    mixed = embed_ref[...].astype(F32) + dot(gated, w_ref[...], ((1,), (0,)))
    out_ref[...] = mixed.astype(BF16)


def finish(returned, place, embed, gate, gain, w_out):
    rows, width = embed.shape
    return pl.pallas_call(
        finish_kernel,
        out_shape=jax.ShapeDtypeStruct((rows, width), BF16),
        in_specs=[vmem()] * 6,
        out_specs=vmem(),
        scratch_shapes=[pltpu.VMEM((rows, width), F32)],
        compiler_params=params(),
        name="finish",
    )(returned, place, embed, gate, gain.reshape(1, width), w_out)


def body(
    cand_embed,
    cand_group,
    cand_user,
    hist_len,
    block_list,
    hist_keys,
    hist_values,
    in_gain,
    w_in,
    attn_gain,
    w_out,
):
    groups = lax.axis_size("user")
    hist_count = lax.axis_size("hist")
    devices = groups * hist_count
    everyone = ("user", "hist")
    blocks_here = block_list.shape[0]

    rows = cand_embed.shape[0]
    me_user = lax.axis_index("user")
    me = me_user * hist_count + lax.axis_index("hist")
    turn = jnp.reshape(me % (HEAD // SLOTS), (1,)).astype(jnp.int32)
    packed, normed, slot = make_queries(
        turn,
        block_list,
        cand_group.reshape(1, rows),
        cand_user.reshape(1, rows),
        cand_embed,
        in_gain,
        w_in,
        groups,
    )
    packed, keys, values, normed = lax.optimization_barrier(
        (packed, hist_keys, hist_values, normed)
    )
    arrived = lax.all_to_all(
        packed.reshape(devices, SLOTS + PAD, HEAD),
        everyone,
        split_axis=0,
        concat_axis=0,
        tiled=True,
    )
    kv = regroup(keys, values)
    gate, place = make_gate(slot, normed, w_in, groups * SLOTS)
    kv, arrived, gate, place = lax.optimization_barrier((kv, arrived, gate, place))
    kv = lax.all_to_all(kv, "hist", split_axis=0, concat_axis=0, tiled=True)

    tags = arrived[:, SLOTS, :].astype(jnp.int32).reshape(-1, HEAD // SLOTS, HEAD)
    tags = jnp.sum(tags, axis=1).reshape(devices * SLOTS // CHUNK, CHUNK)
    counts = jnp.sum(
        tags[:, None, :] == jnp.arange(USERS, dtype=jnp.int32)[None, :, None],
        axis=2,
        dtype=jnp.int32,
    )
    listed = lax.dynamic_slice(
        arrived, (me_user * hist_count, SLOTS + 1, 0), (hist_count, 1, blocks_here)
    )
    listed = listed.astype(jnp.int32).reshape(1, -1)
    order = jnp.arange(hist_count * blocks_here, dtype=jnp.int32)
    where = jnp.sum(jnp.where(listed == order[:, None], order[None, :], 0), axis=1)
    pick, query = sort_queries(counts, tags, arrived)

    attended = attend(counts, where, hist_len, query, pick, kv)
    returned = lax.all_to_all(
        attended.reshape(devices, SLOTS, HEAD), everyone, split_axis=0, concat_axis=0, tiled=True
    )
    return finish(
        returned.reshape(groups, HEADS, SLOTS, HEAD), place, cand_embed, gate, attn_gain, w_out
    )


def solution(mesh):
    split = P(("user", "hist"))
    in_specs = (split, split, split, P("user"), split, split, split, P(), P(), P(), P())
    return jax.shard_map(body, mesh=mesh, in_specs=in_specs, out_specs=split, check_vma=False)
```

profile of v0, /device:TPU:1, one launch (start us, length us, event | category | flops | bytes accessed | tf_op | source)
XLA Modules:
  0.0 150.4 jit_solution(15094418619997501757)
XLA Ops:
  0.0 0.0 copy-start.4
  0.0 1.0 copy-done.4
  1.0 0.0 copy-start.8
  1.0 0.7 copy-done.8
  1.7 0.0 copy-start.10
  1.7 0.7 copy-done.10
  2.4 0.0 copy-start.11
  2.4 0.7 copy-done.11
  3.1 0.0 copy-start.12
  3.1 0.7 copy-done.12
  3.7 5.5 %make_queries.1 = (bf16[16,8,48,128]{3,2,1,0:T(8,128)(2,1)}, bf16[256,1024]{1,0:T(8,128)(2,1)S(1)}, s32[1,256]{1,0:T(1,128)S(1)}) custom-call(s32[1]{0:T(128)} %bitcast.turn_ref, s32[8]{0:T(128)S(1)} %copy-done.12, s32[1,256]{1,0:T(1,128)S(1)} %bitcast.13, s32[1,256]{1,0:T(1,128)S(1)} %bitcast.14, bf16[256,1024]{1,0:T(8,128)(2,1)S(1)} %copy-done.4, ...), custom_call_target="tpu_custom_call" | custom-call | tf_op jit(solution)/shard_map/make_queries/pallas_call | solution.py:130
  9.2 11.5 %all-to-all-start = ((bf16[128,48,128]{2,1,0:T(8,128)(2,1)}), bf16[128,48,128]{2,1,0:T(8,128)(2,1)S(1)}, u32[]{:S(2)}, u32[]{:S(2)}) async-start(bf16[128,48,128]{2,1,0:T(8,128)(2,1)} %bitcast.4), calls=%async_computation | async-start | bytes 3145728 | tf_op jit(solution)/shard_map/all_to_all | solution.py:437
  20.7 0.0 copy-start
  20.7 2.2 %copy-done = bf16[1024,2048]{1,0:T(8,128)(2,1)S(1)} copy-done((bf16[1024,2048]{1,0:T(8,128)(2,1)S(1)}, bf16[1024,2048]{1,0:T(8,128)(2,1)}, u32[]{:S(2)}) %copy-start) | copy-done | bytes 4194328
  22.9 0.0 copy-start.2
  22.9 0.0 copy-start.3
  22.9 0.9 make_gate.1
  23.8 0.0 copy-start.6
  23.8 0.7 copy-done.6
  24.5 0.0 copy-done.2
  24.5 0.7 copy-done.3
  25.2 4.5 %regroup.1 = bf16[8,1024,256]{2,1,0:T(8,128)(2,1)} custom-call(bf16[1024,1024]{1,0:T(8,128)(2,1)S(1)} %copy-done.2, bf16[1024,1024]{1,0:T(8,128)(2,1)S(1)} %copy-done.3), custom_call_target="tpu_custom_call" | custom-call | tf_op jit(solution)/shard_map/regroup/pallas_call | solution.py:52
  29.8 16.0 %all-to-all-done.query_ref = bf16[128,48,128]{2,1,0:T(8,128)(2,1)S(1)} async-done(((bf16[128,48,128]{2,1,0:T(8,128)(2,1)}), bf16[128,48,128]{2,1,0:T(8,128)(2,1)S(1)}, u32[]{:S(2)}, u32[]{:S(2)}) %all-to-all-start) | async-done | bytes 1572896 | tf_op jit(solution)/shard_map/all_to_all | solution.py:437
  45.8 0.0 copy-start.13
  45.8 4.7 %all-to-all-start.1 = ((bf16[8,1024,256]{2,1,0:T(8,128)(2,1)}), bf16[8,1024,256]{2,1,0:T(8,128)(2,1)}, u32[]{:S(2)}, u32[]{:S(2)}) async-start(bf16[8,1024,256]{2,1,0:T(8,128)(2,1)} %regroup.1), calls=%async_computation.1 | async-start | bytes 8388608 | tf_op jit(solution)/shard_map/all_to_all | solution.py:447
  50.5 0.1 reshape.41
  50.6 0.1 slice_convert_fusion
  50.7 0.1 convert_reduce_fusion
  50.8 0.1 copy.13.counts_ref
  50.9 7.5 %sort_queries.1 = (bf16[8,512,640]{2,1,0:T(8,128)(2,1)}, bf16[5376,128]{1,0:T(8,128)(2,1)S(1)}) custom-call(s32[8,4]{1,0:T(8,128)S(1)} %copy.13.counts_ref, s32[8,512]{1,0:T(8,128)S(1)} %eq.35.tags_ref, bf16[128,48,128]{2,1,0:T(8,128)(2,1)S(1)} %all-to-all-done.query_ref), custom_call_target="tpu_custom_call" | custom-call | tf_op jit(solution)/shard_map/sort_queries/pallas_call | solution.py:262
  58.5 0.1 select_reduce_fusion.where_ref
  58.6 42.3 %all-to-all-done.1.kv_hbm = bf16[8,1024,256]{2,1,0:T(8,128)(2,1)} async-done(((bf16[8,1024,256]{2,1,0:T(8,128)(2,1)}), bf16[8,1024,256]{2,1,0:T(8,128)(2,1)}, u32[]{:S(2)}, u32[]{:S(2)}) %all-to-all-start.1) | async-done | bytes 4194336 | tf_op jit(solution)/shard_map/all_to_all | solution.py:447
  100.9 0.0 copy-done.13
  100.9 0.0 copy-start.5
  100.9 0.0 copy-start.7
  100.9 11.3 %attend.1 = bf16[8,512,128]{2,1,0:T(8,128)(2,1)S(1)} custom-call(s32[8,4]{1,0:T(8,128)S(1)} %copy.13.counts_ref, s32[64]{0:T(128)S(1)} %select_reduce_fusion.where_ref, s32[4]{0:T(128)S(1)} %copy-done.13, bf16[5376,128]{1,0:T(8,128)(2,1)S(1)} %get-tuple-element.30.query_ref, bf16[8,512,640]{2,1,0:T(8,128)(2,1)} %get-tuple-element.31.pick_hbm, ...), custom_call_target="tpu_custom_call" | custom-call | tf_op jit(solution)/shard_map/attend/pallas_call | solution.py:357
  112.2 0.0 copy-start.1
  112.2 0.0 copy-start.9
  112.2 35.9 %all_to_all.15 = bf16[128,32,128]{2,1,0:T(8,128)(2,1)S(1)} all-to-all(bf16[128,32,128]{2,1,0:T(8,128)(2,1)S(1)} %bitcast.9), channel_id=1, replica_groups=mesh['user'=16,'hist'=8] {'user','hist'}, dimensions={0} | all-to-all | bytes 2097152 | tf_op jit(solution)/shard_map/all_to_all | solution.py:465
  148.1 0.0 copy-done.5
  148.1 0.0 copy-done.7
  148.1 0.0 copy-done.1
  148.1 0.0 copy-done.9
  148.1 2.2 %finish.1 = bf16[256,1024]{1,0:T(8,128)(2,1)} custom-call(bf16[16,8,32,128]{3,2,1,0:T(8,128)(2,1)S(1)} %bitcast.10, bf16[256,512]{1,0:T(8,128)(2,1)S(1)} %copy-done.7, bf16[256,1024]{1,0:T(8,128)(2,1)S(1)} %copy-done.5, bf16[256,1024]{1,0:T(8,128)(2,1)S(1)} %get-tuple-element.34.gate_ref, f32[1,1024]{1,0:T(1,128)S(1)} %bitcast.12, ...), custom_call_target="tpu_custom_call" | custom-call | tf_op jit(solution)/shard_map/finish/pallas_call | solution.py:390
  (3 shorter events, 0.1 us)
Async XLA Ops:
  0.0 1.0 copy-start.4
  1.0 0.7 copy-start.8
  1.7 0.7 copy-start.10
  2.4 0.7 copy-start.11
  3.1 0.7 copy-start.12
  9.2 36.6 %all-to-all-start = ((bf16[128,48,128]{2,1,0:T(8,128)(2,1)}), bf16[128,48,128]{2,1,0:T(8,128)(2,1)S(1)}, u32[]{:S(2)}, u32[]{:S(2)}) async-start(bf16[128,48,128]{2,1,0:T(8,128)(2,1)} %bitcast.4), calls=%async_computation | async-start | bytes 3145728 | tf_op jit(solution)/shard_map/all_to_all | solution.py:437
  20.7 2.2 %copy-start = (bf16[1024,2048]{1,0:T(8,128)(2,1)S(1)}, bf16[1024,2048]{1,0:T(8,128)(2,1)}, u32[]{:S(2)}) copy-start(bf16[1024,2048]{1,0:T(8,128)(2,1)} %w_ref.4) | copy-start | bytes 12582916
  22.9 1.6 %copy-start.2 = (bf16[1024,1024]{1,0:T(8,128)(2,1)S(1)}, bf16[1024,1024]{1,0:T(8,128)(2,1)}, u32[]{:S(2)}) copy-start(bf16[1024,1024]{1,0:T(8,128)(2,1)} %keys_ref) | copy-start | bytes 6291460
  22.9 2.3 %copy-start.3 = (bf16[1024,1024]{1,0:T(8,128)(2,1)S(1)}, bf16[1024,1024]{1,0:T(8,128)(2,1)}, u32[]{:S(2)}) copy-start(bf16[1024,1024]{1,0:T(8,128)(2,1)} %values_ref) | copy-start | bytes 6291460
  23.8 0.7 copy-start.6
  45.8 55.1 %copy-start.13 = (s32[4]{0:T(128)S(1)}, s32[4]{0:T(128)}, u32[]{:S(2)}) copy-start(s32[4]{0:T(128)} %length_ref.1) | copy-start | bytes 52
  45.8 55.1 %all-to-all-start.1 = ((bf16[8,1024,256]{2,1,0:T(8,128)(2,1)}), bf16[8,1024,256]{2,1,0:T(8,128)(2,1)}, u32[]{:S(2)}, u32[]{:S(2)}) async-start(bf16[8,1024,256]{2,1,0:T(8,128)(2,1)} %regroup.1), calls=%async_computation.1 | async-start | bytes 8388608 | tf_op jit(solution)/shard_map/all_to_all | solution.py:447
  100.9 47.3 %copy-start.5 = (bf16[256,1024]{1,0:T(8,128)(2,1)S(1)}, bf16[256,1024]{1,0:T(8,128)(2,1)}, u32[]{:S(2)}) copy-start(bf16[256,1024]{1,0:T(8,128)(2,1)} %embed_ref.3) | copy-start | bytes 1572868
  100.9 47.3 %copy-start.7 = (bf16[256,512]{1,0:T(8,128)(2,1)S(1)}, bf16[256,512]{1,0:T(8,128)(2,1)}, u32[]{:S(2)}) copy-start(bf16[256,512]{1,0:T(8,128)(2,1)} %copy-done.6) | copy-start | bytes 786436
  112.2 36.0 %copy-start.1 = (bf16[1024,1024]{1,0:T(8,128)(2,1)S(1)}, bf16[1024,1024]{1,0:T(8,128)(2,1)}, u32[]{:S(2)}) copy-start(bf16[1024,1024]{1,0:T(8,128)(2,1)} %w_ref.5) | copy-start | bytes 6291460
  112.2 36.0 %copy-start.9 = (f32[1024]{0:T(1024)S(1)}, f32[1024]{0:T(1024)}, u32[]{:S(2)}) copy-start(f32[1024]{0:T(1024)} %param.20) | copy-start | bytes 12292
where the time goes:
time: 152 us; the launch traced here: 150 us
  waiting for transfers between devices  58.3 us (38%)
  blocking collectives  35.9 us (24%)
  Pallas kernels  31.9 us (21%)
  starting transfers between devices  16.2 us (11%)
  local copies, waits for them, and re-layouts  7.55 us (5%)
    all_to_all x1, waiting for transfers between devices, body(): kv = lax.all_to_all(kv, 'hist', split_axis=0, concat_axis=0, tiled=True)  42.3 us
    all_to_all x1, blocking collectives, body(): lax.all_to_all(attended.reshape(devices, SLOTS, HEAD), everyone, split_ax...  35.9 us
    all_to_all x1, waiting for transfers between devices, body(): lax.all_to_all(packed.reshape(devices, SLOTS + PAD, HEAD), everyone, spli...  16 us
    all_to_all x1, starting transfers between devices, body(): lax.all_to_all(packed.reshape(devices, SLOTS + PAD, HEAD), everyone, spli...  11.5 us
    pallas_call x1, Pallas kernels, attend(): pl.pallas_call(attend_kernel, out_shape=jax.ShapeDtypeStruct((chunks, CHU...  11.3 us
    pallas_call x1, Pallas kernels, sort_queries(): pl.pallas_call(sort_kernel, out_shape=(jax.ShapeDtypeStruct((chunks, CHUN...  7.54 us
    unnamed x28, local copies, waits for them, and re-layouts  7.38 us
    pallas_call x1, Pallas kernels, make_queries(): pl.pallas_call(query_kernel, grid=(width // step,), out_shape=(jax.ShapeD...  5.45 us
  transfers between devices with their start and end apart: 2, of which 2 were waited for; matrix products, arithmetic and copies ran while one was open for 0% of the time, Pallas kernels for 9%

commit v1 on v0

--- a/solution.py
+++ b/solution.py
@@ -14,6 +14,7 @@
 USERS = 4
 SLOTS = 32
 CHUNK = 512
+NOTE = 8
 PAD = 16
 SORTED = CHUNK + 128
 COPY = 64
@@ -62,98 +63,132 @@
 
 def query_kernel(
     turn_ref,
-    list_ref,
+    list_hbm,
+    group_hbm,
+    user_hbm,
+    embed_hbm,
+    gain_hbm,
+    w_hbm,
+    packed_hbm,
+    normed_ref,
+    slot_ref,
+    listed,
     group_ref,
     user_ref,
     embed_ref,
     gain_ref,
     w_ref,
     packed_ref,
-    normed_ref,
-    slot_ref,
-    place,
-    notes,
+    sems,
+    w_sems,
+    out_sems,
 ):
     rows = embed_ref.shape[0]
-    groups = packed_ref.shape[0]
+    groups = packed_hbm.shape[0]
     slots = groups * SLOTS
-
-    @pl.when(pl.program_id(0) == 0)
-    def _():
-        group = group_ref[...]
-        member = (group == lax.broadcasted_iota(jnp.int32, (groups, rows), 0)).astype(F32)
-        before = (
-            lax.broadcasted_iota(jnp.int32, (rows, rows), 0)
-            < lax.broadcasted_iota(jnp.int32, (rows, rows), 1)
-        ).astype(BF16)
-        count = dot(member.astype(BF16), before, ((1,), (0,)))
-        position = jnp.sum(count * member, axis=0, keepdims=True).astype(jnp.int32)
-        slot = group * SLOTS + position
-        slot_ref[...] = slot
-        place[...] = (slot == lax.broadcasted_iota(jnp.int32, (slots, rows), 0)).astype(BF16)
-        offset = turn_ref[0] * SLOTS
-        lanes = lax.broadcasted_iota(jnp.int32, (HEAD, rows), 0) == position + offset
-        users = member * (user_ref[...] - USERS).astype(F32)
-        tags = dot(users.astype(BF16), lanes.astype(BF16), ((1,), (1,)))
-        own = lax.broadcasted_iota(jnp.int32, tags.shape, 1) - offset
-        tags = tags + jnp.where((own >= 0) & (own < SLOTS), USERS, 0).astype(F32)
-        lane = lax.broadcasted_iota(jnp.int32, (groups, PAD, HEAD), 2)
-        row = lax.broadcasted_iota(jnp.int32, (groups, PAD, HEAD), 1)
-        listed = jnp.zeros((groups, PAD, HEAD), jnp.int32)
-        for b in range(list_ref.shape[0]):
-            listed = jnp.where(lane == b, list_ref[b], listed)
-        tags = jnp.broadcast_to(tags.reshape(groups, 1, HEAD), (groups, PAD, HEAD))
-        notes[...] = jnp.where(
-            row == 0, tags, jnp.where(row == 1, listed.astype(F32), 0.0)
-        ).astype(BF16)
-        values = embed_ref[...].astype(F32)
-        scaling = lax.rsqrt(jnp.mean(values * values, axis=-1, keepdims=True) + 1e-06)
-        normed_ref[...] = (values * scaling * gain_ref[...]).astype(BF16)
-
-    query = dot(normed_ref[...], w_ref[...], ((1,), (0,)))
-    query = (query / (1.0 + jnp.exp(-query))).astype(BF16)
-    packed = dot(place[...], query, ((1,), (0,))).astype(BF16)
-    for h in range(packed_ref.shape[1]):
-        packed_ref[:, h, :SLOTS] = packed[:, h * HEAD : (h + 1) * HEAD].reshape(
-            groups, SLOTS, HEAD
+    steps, _, step = w_ref.shape
+    fetches = [
+        pltpu.make_async_copy(source, target, sems.at[i])
+        for i, (source, target) in enumerate(
+            (
+                (group_hbm, group_ref),
+                (user_hbm, user_ref),
+                (embed_hbm, embed_ref),
+                (gain_hbm, gain_ref),
+                (list_hbm, listed),
+            )
         )
-        packed_ref[:, h, SLOTS:] = notes[...]
+    ]
+    for fetch in fetches:
+        fetch.start()
+    blocks = [
+        pltpu.make_async_copy(w_hbm.at[:, pl.ds(i * step, step)], w_ref.at[i], w_sems.at[i])
+        for i in range(steps)
+    ]
+    for block in blocks:
+        block.start()
+
+    fetches[0].wait()
+    group = group_ref[...]
+    member = (group == lax.broadcasted_iota(jnp.int32, (groups, rows), 0)).astype(F32)
+    before = (
+        lax.broadcasted_iota(jnp.int32, (rows, rows), 0)
+        < lax.broadcasted_iota(jnp.int32, (rows, rows), 1)
+    ).astype(BF16)
+    count = dot(member.astype(BF16), before, ((1,), (0,)))
+    position = jnp.sum(count * member, axis=0, keepdims=True).astype(jnp.int32)
+    slot = group * SLOTS + position
+    slot_ref[...] = slot
+    place = (slot == lax.broadcasted_iota(jnp.int32, (slots, rows), 0)).astype(BF16)
+    fetches[1].wait()
+    offset = turn_ref[0] * SLOTS
+    lanes = lax.broadcasted_iota(jnp.int32, (HEAD, rows), 0) == position + offset
+    users = member * (user_ref[...] - USERS).astype(F32)
+    tags = dot(users.astype(BF16), lanes.astype(BF16), ((1,), (1,)))
+    own = lax.broadcasted_iota(jnp.int32, tags.shape, 1) - offset
+    tags = tags + jnp.where((own >= 0) & (own < SLOTS), USERS, 0).astype(F32)
+    fetches[4].wait()
+    lane = lax.broadcasted_iota(jnp.int32, (groups, NOTE, HEAD), 2)
+    row = lax.broadcasted_iota(jnp.int32, (groups, NOTE, HEAD), 1)
+    blocks_here = jnp.zeros((groups, NOTE, HEAD), jnp.int32)
+    for b in range(list_hbm.shape[1]):
+        blocks_here = jnp.where(lane == b, listed[0, b], blocks_here)
+    tags = jnp.broadcast_to(tags.reshape(groups, 1, HEAD), (groups, NOTE, HEAD))
+    notes = jnp.where(
+        row == 0, tags, jnp.where(row == 1, blocks_here.astype(F32), 0.0)
+    ).astype(BF16)
+
+    fetches[2].wait()
+    fetches[3].wait()
+    values = embed_ref[...].astype(F32)
+    scaling = lax.rsqrt(jnp.mean(values * values, axis=-1, keepdims=True) + 1e-06)
+    normed = (values * scaling * gain_ref[...]).astype(BF16)
+    normed_ref[...] = normed
+    stores = []
+    for i in range(steps):
+        blocks[i].wait()
+        query = dot(normed, w_ref[i], ((1,), (0,)))
+        query = (query / (1.0 + jnp.exp(-query))).astype(BF16)
+        packed = dot(place, query, ((1,), (0,))).astype(BF16)
+        for j in range(step // HEAD):
+            h = i * (step // HEAD) + j
+            packed_ref[h, :, :SLOTS] = packed[:, j * HEAD : (j + 1) * HEAD].reshape(
+                groups, SLOTS, HEAD
+            )
+            packed_ref[h, :, SLOTS:] = notes
+            store = pltpu.make_async_copy(packed_ref.at[h], packed_hbm.at[:, h], out_sems.at[h])
+            store.start()
+            stores.append(store)
+    for store in stores:
+        store.wait()
 
 
 def make_queries(turn, listed, group, user, embed, gain, w_in, groups):
     rows, width = embed.shape
     step = 2 * HEAD
-
-    def whole(*shape):
-        return pl.BlockSpec(shape, lambda i: (0,) * len(shape))
-
+    hbm = pl.BlockSpec(memory_space=pltpu.HBM)
     return pl.pallas_call(
         query_kernel,
-        grid=(width // step,),
         out_shape=(
-            jax.ShapeDtypeStruct((groups, HEADS, SLOTS + PAD, HEAD), BF16),
+            jax.ShapeDtypeStruct((groups, HEADS, SLOTS + NOTE, HEAD), BF16),
             jax.ShapeDtypeStruct((rows, width), BF16),
             jax.ShapeDtypeStruct((1, rows), jnp.int32),
         ),
-        in_specs=[
-            smem(),
-            smem(),
-            whole(1, rows),
-            whole(1, rows),
-            whole(rows, width),
-            whole(1, width),
-            pl.BlockSpec((width, step), lambda i: (0, i)),
+        in_specs=[smem()] + [hbm] * 6,
+        out_specs=(hbm, vmem(), vmem()),
+        scratch_shapes=[
+            pltpu.SMEM(listed.shape, jnp.int32),
+            pltpu.VMEM((1, rows), jnp.int32),
+            pltpu.VMEM((1, rows), jnp.int32),
+            pltpu.VMEM((rows, width), BF16),
+            pltpu.VMEM((1, width), F32),
+            pltpu.VMEM((width // step, width, step), BF16),
+            pltpu.VMEM((HEADS, groups, SLOTS + NOTE, HEAD), BF16),
+            pltpu.SemaphoreType.DMA((5,)),
+            pltpu.SemaphoreType.DMA((width // step,)),
+            pltpu.SemaphoreType.DMA((HEADS,)),
         ],
-        out_specs=(
-            pl.BlockSpec((groups, step // HEAD, SLOTS + PAD, HEAD), lambda i: (0, i, 0, 0)),
-            whole(rows, width),
-            whole(1, rows),
-        ),
-        scratch_shapes=[
-            pltpu.VMEM((groups * SLOTS, rows), BF16),
-            pltpu.VMEM((groups, PAD, HEAD), BF16),
-        ],
-        compiler_params=params(),
+        compiler_params=pltpu.CompilerParams(vmem_limit_bytes=64 * 1024 * 1024),
         name="make_queries",
     )(turn, listed, group, user, embed, gain.reshape(1, width), w_in)
 
@@ -423,7 +458,7 @@
     turn = jnp.reshape(me % (HEAD // SLOTS), (1,)).astype(jnp.int32)
     packed, normed, slot = make_queries(
         turn,
-        block_list,
+        block_list.reshape(1, -1),
         cand_group.reshape(1, rows),
         cand_user.reshape(1, rows),
         cand_embed,
@@ -435,7 +470,7 @@
         (packed, hist_keys, hist_values, normed)
     )
     arrived = lax.all_to_all(
-        packed.reshape(devices, SLOTS + PAD, HEAD),
+        packed.reshape(devices, SLOTS + NOTE, HEAD),
         everyone,
         split_axis=0,
         concat_axis=0,

time: 152 us -> 144 us (0.947)
  blocking collectives: 35.9 us -> 26.7 us
  Pallas kernels: 31.9 us -> 40.2 us
  local copies, waits for them, and re-layouts: 7.55 us -> 3.73 us
  waiting for transfers between devices: 58.3 us -> 55.5 us
    all_to_all x1, blocking collectives: 35.9 us -> 26.7 us  [body(): lax.all_to_all(attended.reshape(devices, SLOTS, HEAD), everyone, split_ax...]
    pallas_call x1, Pallas kernels: 11.3 us -> 18.9 us  [attend(): pl.pallas_call(attend_kernel, out_shape=jax.ShapeDtypeStruct((chunks, CHU...]
    unnamed x28 -> x18, local copies, waits for them, and re-layouts: 7.38 us -> 3.57 us
    all_to_all x1, waiting for transfers between devices: 16 us -> 13.3 us  [body(): lax.all_to_all(packed.reshape(devices, SLOTS + NOTE, HEAD), everyone, spl...]
where the time goes in v1:
time: 144 us; the launch traced here: 143 us
  waiting for transfers between devices  55.5 us (39%)
  Pallas kernels  40.2 us (28%)
  blocking collectives  26.7 us (19%)
  starting transfers between devices  16.2 us (11%)
  local copies, waits for them, and re-layouts  3.73 us (3%)
    all_to_all x1, waiting for transfers between devices, body(): kv = lax.all_to_all(kv, 'hist', split_axis=0, concat_axis=0, tiled=True)  42.2 us
    all_to_all x1, blocking collectives, body(): lax.all_to_all(attended.reshape(devices, SLOTS, HEAD), everyone, split_ax...  26.7 us
    pallas_call x1, Pallas kernels, attend(): pl.pallas_call(attend_kernel, out_shape=jax.ShapeDtypeStruct((chunks, CHU...  18.9 us
    all_to_all x1, waiting for transfers between devices, body(): lax.all_to_all(packed.reshape(devices, SLOTS + NOTE, HEAD), everyone, spl...  13.3 us
    all_to_all x1, starting transfers between devices, body(): lax.all_to_all(packed.reshape(devices, SLOTS + NOTE, HEAD), everyone, spl...  11.5 us
    pallas_call x1, Pallas kernels, sort_queries(): pl.pallas_call(sort_kernel, out_shape=(jax.ShapeDtypeStruct((chunks, CHUN...  7.79 us
    pallas_call x1, Pallas kernels, make_queries(): pl.pallas_call(query_kernel, out_shape=(jax.ShapeDtypeStruct((groups, HEA...  5.98 us
    all_to_all x1, starting transfers between devices, body(): kv = lax.all_to_all(kv, 'hist', split_axis=0, concat_axis=0, tiled=True)  4.67 us
  transfers between devices with their start and end apart: 2, of which 2 were waited for; matrix products, arithmetic and copies ran while one was open for 0% of the time, Pallas kernels for 9%

profile of v1, /device:TPU:1, one launch (start us, length us, event | category | flops | bytes accessed | tf_op | source)
XLA Modules:
  0.0 142.9 jit_solution(9827759880406199960)
XLA Ops:
  0.0 6.0 %make_queries.1 = (bf16[16,8,40,128]{3,2,1,0:T(8,128)(2,1)}, bf16[256,1024]{1,0:T(8,128)(2,1)}, s32[1,256]{1,0:T(1,128)}) custom-call(s32[1]{0:T(128)} %bitcast.turn_ref, s32[1,8]{1,0:T(1,128)} %bitcast.18, s32[1,256]{1,0:T(1,128)} %bitcast.16, s32[1,256]{1,0:T(1,128)} %bitcast.17, bf16[256,1024]{1,0:T(8,128)(2,1)} %embed_ref.1, f32[1,1024]{1,0:T(1,128)} %bitcast.15, ...), custom_call_target="tpu_custom_call" | custom-call | tf_op jit(solution)/shard_map/make_queries/pallas_call | solution.py:170
  6.0 0.0 copy-start.5
  6.0 0.0 copy-start.7
  6.0 11.5 %all-to-all-start = ((bf16[128,40,128]{2,1,0:T(8,128)(2,1)}), bf16[128,40,128]{2,1,0:T(8,128)(2,1)S(1)}, u32[]{:S(2)}, u32[]{:S(2)}) async-start(bf16[128,40,128]{2,1,0:T(8,128)(2,1)} %bitcast.13), calls=%async_computation | async-start | bytes 2621440 | tf_op jit(solution)/shard_map/all_to_all | solution.py:472
  17.5 0.0 copy-done.5
  17.5 0.0 copy-done.7
  17.5 0.0 copy-start
  17.6 2.2 %copy-done = bf16[1024,2048]{1,0:T(8,128)(2,1)S(1)} copy-done((bf16[1024,2048]{1,0:T(8,128)(2,1)S(1)}, bf16[1024,2048]{1,0:T(8,128)(2,1)}, u32[]{:S(2)}) %copy-start) | copy-done | bytes 4194328
  19.7 0.0 copy-start.2
  19.7 0.0 copy-start.3
  19.7 0.9 make_gate.1
  20.6 0.7 copy-done.2
  21.3 0.6 copy-done.3
  22.0 4.5 %regroup.1 = bf16[8,1024,256]{2,1,0:T(8,128)(2,1)} custom-call(bf16[1024,1024]{1,0:T(8,128)(2,1)S(1)} %copy-done.2, bf16[1024,1024]{1,0:T(8,128)(2,1)S(1)} %copy-done.3), custom_call_target="tpu_custom_call" | custom-call | tf_op jit(solution)/shard_map/regroup/pallas_call | solution.py:53
  26.5 13.3 %all-to-all-done.query_ref = bf16[128,40,128]{2,1,0:T(8,128)(2,1)S(1)} async-done(((bf16[128,40,128]{2,1,0:T(8,128)(2,1)}), bf16[128,40,128]{2,1,0:T(8,128)(2,1)S(1)}, u32[]{:S(2)}, u32[]{:S(2)}) %all-to-all-start) | async-done | bytes 1310752 | tf_op jit(solution)/shard_map/all_to_all | solution.py:472
  39.8 0.0 copy-start.8
  39.8 4.7 %all-to-all-start.1 = ((bf16[8,1024,256]{2,1,0:T(8,128)(2,1)}), bf16[8,1024,256]{2,1,0:T(8,128)(2,1)}, u32[]{:S(2)}, u32[]{:S(2)}) async-start(bf16[8,1024,256]{2,1,0:T(8,128)(2,1)} %regroup.1), calls=%async_computation.1 | async-start | bytes 8388608 | tf_op jit(solution)/shard_map/all_to_all | solution.py:482
  44.5 0.1 reshape.45
  44.6 0.1 slice_convert_fusion
  44.7 0.1 convert_reduce_fusion
  44.9 0.1 copy.13.counts_ref
  44.9 7.8 %sort_queries.1 = (bf16[8,512,640]{2,1,0:T(8,128)(2,1)}, bf16[5376,128]{1,0:T(8,128)(2,1)S(1)}) custom-call(s32[8,4]{1,0:T(8,128)S(1)} %copy.13.counts_ref, s32[8,512]{1,0:T(8,128)S(1)} %eq.35.tags_ref, bf16[128,40,128]{2,1,0:T(8,128)(2,1)S(1)} %all-to-all-done.query_ref), custom_call_target="tpu_custom_call" | custom-call | tf_op jit(solution)/shard_map/sort_queries/pallas_call | solution.py:297
  52.7 0.1 select_reduce_fusion.where_ref
  52.8 42.2 %all-to-all-done.1.kv_hbm = bf16[8,1024,256]{2,1,0:T(8,128)(2,1)} async-done(((bf16[8,1024,256]{2,1,0:T(8,128)(2,1)}), bf16[8,1024,256]{2,1,0:T(8,128)(2,1)}, u32[]{:S(2)}, u32[]{:S(2)}) %all-to-all-start.1) | async-done | bytes 4194336 | tf_op jit(solution)/shard_map/all_to_all | solution.py:482
  95.0 0.0 copy-done.8
  95.0 0.0 copy-start.4
  95.0 18.9 %attend.1 = bf16[8,512,128]{2,1,0:T(8,128)(2,1)S(1)} custom-call(s32[8,4]{1,0:T(8,128)S(1)} %copy.13.counts_ref, s32[64]{0:T(128)S(1)} %select_reduce_fusion.where_ref, s32[4]{0:T(128)S(1)} %copy-done.8, bf16[5376,128]{1,0:T(8,128)(2,1)S(1)} %get-tuple-element.30.query_ref, bf16[8,512,640]{2,1,0:T(8,128)(2,1)} %get-tuple-element.31.pick_hbm, ...), custom_call_target="tpu_custom_call" | custom-call | tf_op jit(solution)/shard_map/attend/pallas_call | solution.py:392
  113.9 0.0 copy-start.1
  113.9 0.0 copy-start.6
  113.9 26.7 %all_to_all.15 = bf16[128,32,128]{2,1,0:T(8,128)(2,1)S(1)} all-to-all(bf16[128,32,128]{2,1,0:T(8,128)(2,1)S(1)} %bitcast.10), channel_id=1, replica_groups=mesh['user'=16,'hist'=8] {'user','hist'}, dimensions={0} | all-to-all | bytes 2097152 | tf_op jit(solution)/shard_map/all_to_all | solution.py:500
  140.6 0.0 copy-done.4
  140.6 0.0 copy-done.1
  140.6 0.0 copy-done.6
  140.6 2.2 %finish.1 = bf16[256,1024]{1,0:T(8,128)(2,1)} custom-call(bf16[16,8,32,128]{3,2,1,0:T(8,128)(2,1)S(1)} %bitcast.11, bf16[256,512]{1,0:T(8,128)(2,1)S(1)} %get-tuple-element.33.place_ref, bf16[256,1024]{1,0:T(8,128)(2,1)S(1)} %copy-done.4, bf16[256,1024]{1,0:T(8,128)(2,1)S(1)} %get-tuple-element.34.gate_ref, f32[1,1024]{1,0:T(1,128)S(1)} %bitcast.12, ...), custom_call_target="tpu_custom_call" | custom-call | tf_op jit(solution)/shard_map/finish/pallas_call | solution.py:425
  (3 shorter events, 0.1 us)
Async XLA Ops:
  6.0 11.5 %copy-start.5 = (bf16[256,1024]{1,0:T(8,128)(2,1)S(1)}, bf16[256,1024]{1,0:T(8,128)(2,1)}, u32[]{:S(2)}) copy-start(bf16[256,1024]{1,0:T(8,128)(2,1)} %get-tuple-element.26.normed_ref) | copy-start | bytes 1572868
  6.0 11.5 %copy-start.7 = (s32[1,256]{1,0:T(1,128)S(1)}, s32[1,256]{1,0:T(1,128)}, u32[]{:S(2)}) copy-start(s32[1,256]{1,0:T(1,128)} %get-tuple-element.25.slot_ref) | copy-start | bytes 3076
  6.0 33.8 %all-to-all-start = ((bf16[128,40,128]{2,1,0:T(8,128)(2,1)}), bf16[128,40,128]{2,1,0:T(8,128)(2,1)S(1)}, u32[]{:S(2)}, u32[]{:S(2)}) async-start(bf16[128,40,128]{2,1,0:T(8,128)(2,1)} %bitcast.13), calls=%async_computation | async-start | bytes 2621440 | tf_op jit(solution)/shard_map/all_to_all | solution.py:472
  17.5 2.2 %copy-start = (bf16[1024,2048]{1,0:T(8,128)(2,1)S(1)}, bf16[1024,2048]{1,0:T(8,128)(2,1)}, u32[]{:S(2)}) copy-start(bf16[1024,2048]{1,0:T(8,128)(2,1)} %w_ref.2) | copy-start | bytes 12582916
  19.7 1.6 %copy-start.2 = (bf16[1024,1024]{1,0:T(8,128)(2,1)S(1)}, bf16[1024,1024]{1,0:T(8,128)(2,1)}, u32[]{:S(2)}) copy-start(bf16[1024,1024]{1,0:T(8,128)(2,1)} %keys_ref) | copy-start | bytes 6291460
  19.7 2.2 %copy-start.3 = (bf16[1024,1024]{1,0:T(8,128)(2,1)S(1)}, bf16[1024,1024]{1,0:T(8,128)(2,1)}, u32[]{:S(2)}) copy-start(bf16[1024,1024]{1,0:T(8,128)(2,1)} %values_ref) | copy-start | bytes 6291460
  39.8 55.2 %copy-start.8 = (s32[4]{0:T(128)S(1)}, s32[4]{0:T(128)}, u32[]{:S(2)}) copy-start(s32[4]{0:T(128)} %length_ref.1) | copy-start | bytes 52
  39.8 55.2 %all-to-all-start.1 = ((bf16[8,1024,256]{2,1,0:T(8,128)(2,1)}), bf16[8,1024,256]{2,1,0:T(8,128)(2,1)}, u32[]{:S(2)}, u32[]{:S(2)}) async-start(bf16[8,1024,256]{2,1,0:T(8,128)(2,1)} %regroup.1), calls=%async_computation.1 | async-start | bytes 8388608 | tf_op jit(solution)/shard_map/all_to_all | solution.py:482
  95.0 45.6 %copy-start.4 = (bf16[256,1024]{1,0:T(8,128)(2,1)S(1)}, bf16[256,1024]{1,0:T(8,128)(2,1)}, u32[]{:S(2)}) copy-start(bf16[256,1024]{1,0:T(8,128)(2,1)} %embed_ref.1) | copy-start | bytes 1572868
  113.9 26.7 %copy-start.1 = (bf16[1024,1024]{1,0:T(8,128)(2,1)S(1)}, bf16[1024,1024]{1,0:T(8,128)(2,1)}, u32[]{:S(2)}) copy-start(bf16[1024,1024]{1,0:T(8,128)(2,1)} %w_ref.3) | copy-start | bytes 6291460
  113.9 26.7 %copy-start.6 = (f32[1024]{0:T(1024)S(1)}, f32[1024]{0:T(1024)}, u32[]{:S(2)}) copy-start(f32[1024]{0:T(1024)} %param.20) | copy-start | bytes 12292

commit v2 on v1

--- a/solution.py
+++ b/solution.py
@@ -18,7 +18,8 @@
 PAD = 16
 SORTED = CHUNK + 128
 COPY = 64
-TILE = 256
+TILES = (256, 384, 512, 640, 768)
+TILE = TILES[-1]
 KEYS = 1024
 REST = 512
 VMEM = 48 * 1024 * 1024
@@ -320,6 +321,8 @@
     pick,
     total,
     chunk,
+    start_ref,
+    size_ref,
     kv_sem,
     pick_sem,
 ):
@@ -328,11 +331,11 @@
     starts, sizes = bases(counts_ref, chunks)
     fetch = pltpu.make_async_copy(kv_hbm, kv, kv_sem)
     fetch.start()
-    picks = pltpu.make_async_copy(pick_hbm, pick, pick_sem)
-    picks.start()
     total[...] = jnp.zeros_like(total)
     chunk[...] = jnp.zeros_like(chunk)
     fetch.wait()
+    picks = pltpu.make_async_copy(pick_hbm, pick, pick_sem)
+    picks.start()
 
     scale = 0.5 * HEAD ** (-0.5)
 
@@ -350,28 +353,45 @@
             weight = jnp.where(column < limit, weight, 0.0)
         return dot(weight.astype(BF16), part[:, HEAD:], ((1,), (0,)))
 
-    for u in range(USERS):
+    def attend_tile(size, u, at):
         length = length_ref[u]
         whole = length // KEYS
         rest = (length - whole * KEYS + (REST - 1)) // REST
-
-        def tile(i, carry, u=u, length=length, whole=whole, rest=rest):
-            at = pl.multiple_of(starts[u] + i * TILE, PAD)
-            query = query_ref[pl.ds(at, TILE), :]
-
-            def step(k, running):
-                return running + partial(query, u, k * (KEYS // BLK), KEYS // BLK, None)
-
-            def end(k, running):
-                first = whole * KEYS + k * REST
-                return running + partial(query, u, first // BLK, REST // BLK, length - first)
-
-            running = lax.fori_loop(0, whole, step, jnp.zeros((TILE, HEAD), F32))
-            running = lax.fori_loop(0, rest, end, running)
-            total[pl.ds(at, TILE), :] = running.astype(BF16)
-            return carry
-
-        lax.fori_loop(0, (sizes[u] + (TILE - 1)) // TILE, tile, 0)
+        query = query_ref[pl.ds(at, size), :]
+
+        def step(k, running):
+            return running + partial(query, u, k * (KEYS // BLK), KEYS // BLK, None)
+
+        def end(k, running):
+            first = whole * KEYS + k * REST
+            return running + partial(query, u, first // BLK, REST // BLK, length - first)
+
+        running = lax.fori_loop(0, whole, step, jnp.zeros((size, HEAD), F32))
+        running = lax.fori_loop(0, rest, end, running)
+        total[pl.ds(at, size), :] = running.astype(BF16)
+
+    for u in range(USERS):
+        start_ref[u] = starts[u]
+        size_ref[u] = sizes[u]
+
+    def attend_user(u, carry):
+        def attend_rows(state):
+            at, left = state
+            for shorter, size in zip((0,) + TILES[:-1], TILES):
+                fits = left > shorter
+                if size < TILE:
+                    fits = fits & (left <= size)
+
+                @pl.when(fits)
+                def _(size=size):
+                    attend_tile(size, u, pl.multiple_of(at, PAD))
+
+            return at + TILE, left - TILE
+
+        lax.while_loop(lambda state: state[1] > 0, attend_rows, (start_ref[u], size_ref[u]))
+        return carry
+
+    lax.fori_loop(0, USERS, attend_user, 0)
 
     picks.wait()
     rows = list(starts)
@@ -382,7 +402,13 @@
             copy_rows(count, total, rows[u], chunk, c * SORTED + run[u])
             rows[u] = rows[u] + padded(count)
     for c in range(chunks):
-        out_ref[c] = dot(pick[c], chunk[c * SORTED : (c + 1) * SORTED, :], ((1,), (0,))).astype(BF16)
+        used = runs(counts_ref, c)[USERS - 1] + counts_ref[c, USERS - 1]
+        for shorter, size in ((0, 256), (256, 512), (512, SORTED)):
+
+            @pl.when((used > shorter) & (used <= size) if shorter else used <= size)
+            def _(c=c, size=size):
+                rows = chunk[c * SORTED : c * SORTED + size, :]
+                out_ref[c] = dot(pick[c, :, :size], rows, ((1,), (0,))).astype(BF16)
 
 
 def attend(counts, where, length, query, pick, kv):
@@ -399,6 +425,8 @@
             pltpu.VMEM(pick.shape, BF16),
             pltpu.VMEM((rows, HEAD), BF16),
             pltpu.VMEM((chunks * SORTED + COPY, HEAD), BF16),
+            pltpu.SMEM((USERS,), jnp.int32),
+            pltpu.SMEM((USERS,), jnp.int32),
             pltpu.SemaphoreType.DMA,
             pltpu.SemaphoreType.DMA,
         ],

time: 144 us -> 142 us (0.986)
  Pallas kernels: 40.2 us -> 31.9 us
  blocking collectives: 26.7 us -> 32.7 us
    pallas_call x1, Pallas kernels: 18.9 us -> 10.6 us  [attend(): pl.pallas_call(attend_kernel, out_shape=jax.ShapeDtypeStruct((chunks, CHU...]
    all_to_all x1, blocking collectives: 26.7 us -> 32.7 us  [body(): lax.all_to_all(attended.reshape(devices, SLOTS, HEAD), everyone, split_ax...]
    unnamed x18 -> x22, local copies, waits for them, and re-layouts: 3.57 us -> 3.65 us
where the time goes in v2:
time: 142 us; the launch traced here: 141 us
  waiting for transfers between devices  55.4 us (39%)
  blocking collectives  32.7 us (23%)
  Pallas kernels  31.9 us (22%)
  starting transfers between devices  16.2 us (11%)
  local copies, waits for them, and re-layouts  3.82 us (3%)
    all_to_all x1, waiting for transfers between devices, body(): kv = lax.all_to_all(kv, 'hist', split_axis=0, concat_axis=0, tiled=True)  42.2 us
    all_to_all x1, blocking collectives, body(): lax.all_to_all(attended.reshape(devices, SLOTS, HEAD), everyone, split_ax...  32.7 us
    all_to_all x1, waiting for transfers between devices, body(): lax.all_to_all(packed.reshape(devices, SLOTS + NOTE, HEAD), everyone, spl...  13.2 us
    all_to_all x1, starting transfers between devices, body(): lax.all_to_all(packed.reshape(devices, SLOTS + NOTE, HEAD), everyone, spl...  11.5 us
    pallas_call x1, Pallas kernels, attend(): pl.pallas_call(attend_kernel, out_shape=jax.ShapeDtypeStruct((chunks, CHU...  10.6 us
    pallas_call x1, Pallas kernels, sort_queries(): pl.pallas_call(sort_kernel, out_shape=(jax.ShapeDtypeStruct((chunks, CHUN...  7.76 us
    pallas_call x1, Pallas kernels, make_queries(): pl.pallas_call(query_kernel, out_shape=(jax.ShapeDtypeStruct((groups, HEA...  5.97 us
    all_to_all x1, starting transfers between devices, body(): kv = lax.all_to_all(kv, 'hist', split_axis=0, concat_axis=0, tiled=True)  4.68 us
  transfers between devices with their start and end apart: 2, of which 2 were waited for; matrix products, arithmetic and copies ran while one was open for 0% of the time, Pallas kernels for 9%

profile of v2, /device:TPU:1, one launch (start us, length us, event | category | flops | bytes accessed | tf_op | source)
XLA Modules:
  0.0 140.6 jit_solution(6183061479521801095)
XLA Ops:
  0.0 6.0 %make_queries.1 = (bf16[16,8,40,128]{3,2,1,0:T(8,128)(2,1)}, bf16[256,1024]{1,0:T(8,128)(2,1)}, s32[1,256]{1,0:T(1,128)}) custom-call(s32[1]{0:T(128)} %bitcast.turn_ref, s32[1,8]{1,0:T(1,128)} %bitcast.18, s32[1,256]{1,0:T(1,128)} %bitcast.16, s32[1,256]{1,0:T(1,128)} %bitcast.17, bf16[256,1024]{1,0:T(8,128)(2,1)} %embed_ref.1, f32[1,1024]{1,0:T(1,128)} %bitcast.15, ...), custom_call_target="tpu_custom_call" | custom-call | tf_op jit(solution)/shard_map/make_queries/pallas_call | solution.py:171
  6.0 0.0 copy-start.5
  6.0 0.0 copy-start.9
  6.0 11.5 %all-to-all-start = ((bf16[128,40,128]{2,1,0:T(8,128)(2,1)}), bf16[128,40,128]{2,1,0:T(8,128)(2,1)S(1)}, u32[]{:S(2)}, u32[]{:S(2)}) async-start(bf16[128,40,128]{2,1,0:T(8,128)(2,1)} %bitcast.13), calls=%async_computation | async-start | bytes 2621440 | tf_op jit(solution)/shard_map/all_to_all | solution.py:500
  17.5 0.0 copy-done.5
  17.5 0.0 copy-done.9
  17.5 0.0 copy-start
  17.5 2.2 %copy-done = bf16[1024,2048]{1,0:T(8,128)(2,1)S(1)} copy-done((bf16[1024,2048]{1,0:T(8,128)(2,1)S(1)}, bf16[1024,2048]{1,0:T(8,128)(2,1)}, u32[]{:S(2)}) %copy-start) | copy-done | bytes 4194328
  19.7 0.0 copy-start.2
  19.7 0.0 copy-start.3
  19.7 0.9 make_gate.1
  20.6 0.0 copy-start.6
  20.6 0.7 copy-done.6
  21.3 0.0 copy-done.2
  21.3 0.7 copy-done.3
  22.0 4.5 %regroup.1 = bf16[8,1024,256]{2,1,0:T(8,128)(2,1)} custom-call(bf16[1024,1024]{1,0:T(8,128)(2,1)S(1)} %copy-done.2, bf16[1024,1024]{1,0:T(8,128)(2,1)S(1)} %copy-done.3), custom_call_target="tpu_custom_call" | custom-call | tf_op jit(solution)/shard_map/regroup/pallas_call | solution.py:54
  26.6 13.2 %all-to-all-done.query_ref = bf16[128,40,128]{2,1,0:T(8,128)(2,1)S(1)} async-done(((bf16[128,40,128]{2,1,0:T(8,128)(2,1)}), bf16[128,40,128]{2,1,0:T(8,128)(2,1)S(1)}, u32[]{:S(2)}, u32[]{:S(2)}) %all-to-all-start) | async-done | bytes 1310752 | tf_op jit(solution)/shard_map/all_to_all | solution.py:500
  39.8 0.0 copy-start.10
  39.8 4.7 %all-to-all-start.1 = ((bf16[8,1024,256]{2,1,0:T(8,128)(2,1)}), bf16[8,1024,256]{2,1,0:T(8,128)(2,1)}, u32[]{:S(2)}, u32[]{:S(2)}) async-start(bf16[8,1024,256]{2,1,0:T(8,128)(2,1)} %regroup.1), calls=%async_computation.1 | async-start | bytes 8388608 | tf_op jit(solution)/shard_map/all_to_all | solution.py:510
  44.5 0.1 reshape.45
  44.6 0.1 slice_convert_fusion
  44.7 0.1 convert_reduce_fusion
  44.8 0.1 copy.13.counts_ref
  44.9 7.8 %sort_queries.1 = (bf16[8,512,640]{2,1,0:T(8,128)(2,1)}, bf16[5888,128]{1,0:T(8,128)(2,1)S(1)}) custom-call(s32[8,4]{1,0:T(8,128)S(1)} %copy.13.counts_ref, s32[8,512]{1,0:T(8,128)S(1)} %eq.35.tags_ref, bf16[128,40,128]{2,1,0:T(8,128)(2,1)S(1)} %all-to-all-done.query_ref), custom_call_target="tpu_custom_call" | custom-call | tf_op jit(solution)/shard_map/sort_queries/pallas_call | solution.py:298
  52.7 0.1 select_reduce_fusion.where_ref
  52.8 42.2 %all-to-all-done.1.kv_hbm = bf16[8,1024,256]{2,1,0:T(8,128)(2,1)} async-done(((bf16[8,1024,256]{2,1,0:T(8,128)(2,1)}), bf16[8,1024,256]{2,1,0:T(8,128)(2,1)}, u32[]{:S(2)}, u32[]{:S(2)}) %all-to-all-start.1) | async-done | bytes 4194336 | tf_op jit(solution)/shard_map/all_to_all | solution.py:510
  95.0 0.0 copy-done.10
  95.0 0.0 copy-start.4
  95.0 0.0 copy-start.7
  95.0 10.6 %attend.1 = bf16[8,512,128]{2,1,0:T(8,128)(2,1)S(1)} custom-call(s32[8,4]{1,0:T(8,128)S(1)} %copy.13.counts_ref, s32[64]{0:T(128)S(1)} %select_reduce_fusion.where_ref, s32[4]{0:T(128)S(1)} %copy-done.10, bf16[5888,128]{1,0:T(8,128)(2,1)S(1)} %get-tuple-element.30.query_ref, bf16[8,512,640]{2,1,0:T(8,128)(2,1)} %get-tuple-element.31.pick_hbm, ...), custom_call_target="tpu_custom_call" | custom-call | tf_op jit(solution)/shard_map/attend/pallas_call | solution.py:418
  105.6 0.0 copy-start.1
  105.6 0.0 copy-start.8
  105.6 32.7 %all_to_all.15 = bf16[128,32,128]{2,1,0:T(8,128)(2,1)S(1)} all-to-all(bf16[128,32,128]{2,1,0:T(8,128)(2,1)S(1)} %bitcast.10), channel_id=1, replica_groups=mesh['user'=16,'hist'=8] {'user','hist'}, dimensions={0} | all-to-all | bytes 2097152 | tf_op jit(solution)/shard_map/all_to_all | solution.py:528
  138.3 0.0 copy-done.4
  138.3 0.0 copy-done.7
  138.3 0.0 copy-done.1
  138.3 0.0 copy-done.8
  138.4 2.2 %finish.1 = bf16[256,1024]{1,0:T(8,128)(2,1)} custom-call(bf16[16,8,32,128]{3,2,1,0:T(8,128)(2,1)S(1)} %bitcast.11, bf16[256,512]{1,0:T(8,128)(2,1)S(1)} %copy-done.7, bf16[256,1024]{1,0:T(8,128)(2,1)S(1)} %copy-done.4, bf16[256,1024]{1,0:T(8,128)(2,1)S(1)} %get-tuple-element.34.gate_ref, f32[1,1024]{1,0:T(1,128)S(1)} %bitcast.12, ...), custom_call_target="tpu_custom_call" | custom-call | tf_op jit(solution)/shard_map/finish/pallas_call | solution.py:453
  (3 shorter events, 0.1 us)
Async XLA Ops:
  6.0 11.5 %copy-start.5 = (bf16[256,1024]{1,0:T(8,128)(2,1)S(1)}, bf16[256,1024]{1,0:T(8,128)(2,1)}, u32[]{:S(2)}) copy-start(bf16[256,1024]{1,0:T(8,128)(2,1)} %get-tuple-element.26.normed_ref) | copy-start | bytes 1572868
  6.0 11.5 %copy-start.9 = (s32[1,256]{1,0:T(1,128)S(1)}, s32[1,256]{1,0:T(1,128)}, u32[]{:S(2)}) copy-start(s32[1,256]{1,0:T(1,128)} %get-tuple-element.25.slot_ref) | copy-start | bytes 3076
  6.0 33.8 %all-to-all-start = ((bf16[128,40,128]{2,1,0:T(8,128)(2,1)}), bf16[128,40,128]{2,1,0:T(8,128)(2,1)S(1)}, u32[]{:S(2)}, u32[]{:S(2)}) async-start(bf16[128,40,128]{2,1,0:T(8,128)(2,1)} %bitcast.13), calls=%async_computation | async-start | bytes 2621440 | tf_op jit(solution)/shard_map/all_to_all | solution.py:500
  17.5 2.2 %copy-start = (bf16[1024,2048]{1,0:T(8,128)(2,1)S(1)}, bf16[1024,2048]{1,0:T(8,128)(2,1)}, u32[]{:S(2)}) copy-start(bf16[1024,2048]{1,0:T(8,128)(2,1)} %w_ref.2) | copy-start | bytes 12582916
  19.7 1.6 %copy-start.2 = (bf16[1024,1024]{1,0:T(8,128)(2,1)S(1)}, bf16[1024,1024]{1,0:T(8,128)(2,1)}, u32[]{:S(2)}) copy-start(bf16[1024,1024]{1,0:T(8,128)(2,1)} %keys_ref) | copy-start | bytes 6291460
  19.7 2.3 %copy-start.3 = (bf16[1024,1024]{1,0:T(8,128)(2,1)S(1)}, bf16[1024,1024]{1,0:T(8,128)(2,1)}, u32[]{:S(2)}) copy-start(bf16[1024,1024]{1,0:T(8,128)(2,1)} %values_ref) | copy-start | bytes 6291460
  20.6 0.7 copy-start.6
  39.8 55.2 %copy-start.10 = (s32[4]{0:T(128)S(1)}, s32[4]{0:T(128)}, u32[]{:S(2)}) copy-start(s32[4]{0:T(128)} %length_ref.1) | copy-start | bytes 52
  39.8 55.2 %all-to-all-start.1 = ((bf16[8,1024,256]{2,1,0:T(8,128)(2,1)}), bf16[8,1024,256]{2,1,0:T(8,128)(2,1)}, u32[]{:S(2)}, u32[]{:S(2)}) async-start(bf16[8,1024,256]{2,1,0:T(8,128)(2,1)} %regroup.1), calls=%async_computation.1 | async-start | bytes 8388608 | tf_op jit(solution)/shard_map/all_to_all | solution.py:510
  95.0 43.3 %copy-start.4 = (bf16[256,1024]{1,0:T(8,128)(2,1)S(1)}, bf16[256,1024]{1,0:T(8,128)(2,1)}, u32[]{:S(2)}) copy-start(bf16[256,1024]{1,0:T(8,128)(2,1)} %embed_ref.1) | copy-start | bytes 1572868
  95.0 43.3 %copy-start.7 = (bf16[256,512]{1,0:T(8,128)(2,1)S(1)}, bf16[256,512]{1,0:T(8,128)(2,1)}, u32[]{:S(2)}) copy-start(bf16[256,512]{1,0:T(8,128)(2,1)} %copy-done.6) | copy-start | bytes 786436
  105.6 32.7 %copy-start.1 = (bf16[1024,1024]{1,0:T(8,128)(2,1)S(1)}, bf16[1024,1024]{1,0:T(8,128)(2,1)}, u32[]{:S(2)}) copy-start(bf16[1024,1024]{1,0:T(8,128)(2,1)} %w_ref.3) | copy-start | bytes 6291460
  105.6 32.7 %copy-start.8 = (f32[1024]{0:T(1024)S(1)}, f32[1024]{0:T(1024)}, u32[]{:S(2)}) copy-start(f32[1024]{0:T(1024)} %param.20) | copy-start | bytes 12292
